TPU v7x, 768 devices: a whole 4x8x12 slice. The times are simulated.
768 devices in a mesh: gx: 96 (over y, z), gy: 8 (over x, core).
Axes of the slice: x: 4, y: 8, z: 12, core: 2. Of those that a mesh axis runs over, the one named last changes fastest.
Arguments:
- members: bfloat16 [6144, 512, 128], P('gx', 'gy'), may hold values from -6 to 6
- courant: float32 [2, 6144, 512], P(None, 'gx', 'gy'), may hold values from -0.4 to 0.4
- obs_cells: int32 [96, 8, 128], P('gx', 'gy'), may hold values from 0 to 4095
- obs_count: int32 [96, 8], P('gx', 'gy'), may hold values from 64 to 128, as said below
- obs_value: float32 [96, 8, 128], P('gx', 'gy'), may hold values from -6 to 6
- obs_weight: float32 [96, 8, 128], P('gx', 'gy'), may hold values from 0.5 to 4
Outputs:
- analysis_mean: float32 [6144, 512], P('gx', 'gy')
- analysis_anomalies: bfloat16 [6144, 512, 128], P('gx', 'gy')
Inputs may be any that keep to these rules, and one draw needn't show every extreme that they name: The first obs_count slots of each tile are live; some tile has all 128 live, some tile exactly 64.
All inputs are finite; a program needn't handle non-finite values.
Results may differ from a plain program's by a relative error of at most 0.001.
Values sent between devices are 32-bit elements; how exact they have to be, the bound alone decides.
A program may use at most 32 MiB of HBM per device.

v0:
```python
import math

import jax
import jax.numpy as jnp
from jax import lax
from jax.sharding import PartitionSpec as P

STEPS = 3


diffusion = 0.2


def padded(block, sides, width):
    for axis, dim in sides:
        count = lax.axis_size(axis)
        forward = [(i, i + 1) for i in range(count - 1)]
        backward = [(target, source) for source, target in forward]
        low = lax.ppermute(
            lax.slice_in_dim(block, block.shape[dim] - width, None, axis=dim), axis, forward
        )
        high = lax.ppermute(lax.slice_in_dim(block, 0, width, axis=dim), axis, backward)
        block = jnp.concatenate([low, block, high], axis=dim)
    return block


def advance(padded_field, courant_part):
    centre = padded_field[1:-1, 1:-1]
    east_side = padded_field[2:, 1:-1]
    west_side = padded_field[:-2, 1:-1]
    north_side = padded_field[1:-1, 2:]
    south_side = padded_field[1:-1, :-2]
    return (
        centre
        + diffusion * (east_side + west_side + north_side + south_side - 4.0 * centre)
        - 0.5 * courant_part[0][..., None] * (east_side - west_side)
        - 0.5 * courant_part[1][..., None] * (north_side - south_side)
    )


def shards(members, courant, obs_cells, obs_count, obs_value, obs_weight):
    tile_rows, tile_cols, member_total = members.shape
    ensemble = members.astype(jnp.float32)
    for rotation_index in range(STEPS):
        padded_field = padded(ensemble, (("gx", 0), ("gy", 1)), 1)
        ensemble = advance(padded_field, courant)
    ensemble_average = jnp.sum(ensemble, axis=2) / member_total
    anomaly = ensemble - ensemble_average[..., None]
    flat_anomaly = anomaly.reshape(tile_rows * tile_cols, member_total)
    obs_rows = obs_cells.reshape(-1)
    slot_total = obs_rows.shape[0]
    observed = flat_anomaly[obs_rows]
    obs_mean = ensemble_average.reshape(-1)[obs_rows]
    active_buffer_slot = jnp.arange(slot_total, dtype=jnp.int32) < obs_count[0, 0]
    weight_flat = obs_weight.reshape(-1)
    all_slots = slot_total * lax.axis_size("gx") * lax.axis_size("gy")
    scale_factor = weight_flat / math.sqrt(all_slots)
    scaled = jnp.where(active_buffer_slot[:, None], scale_factor[:, None] * observed, 0.0)
    innovation = jnp.where(
        active_buffer_slot, weight_flat * (obs_value.reshape(-1) - obs_mean), 0.0
    )
    gram_term = jnp.dot(scaled.T, scaled, precision=lax.Precision.HIGHEST)
    cross_term = jnp.dot(scaled.T, innovation, precision=lax.Precision.HIGHEST)
    gram_term, cross_term = lax.psum((gram_term, cross_term), ("gx", "gy"))
    gram_total = gram_term + jnp.eye(member_total, dtype=jnp.float32)
    lower_factor = jnp.linalg.cholesky(gram_total)
    weights = jax.scipy.linalg.cho_solve((lower_factor, True), cross_term)
    analysis_mean = ensemble_average + jnp.dot(
        flat_anomaly, weights, precision=lax.Precision.HIGHEST
    ).reshape(tile_rows, tile_cols)
    solved = jax.scipy.linalg.solve_triangular(lower_factor, flat_anomaly.T, lower=True).T.astype(
        jnp.bfloat16
    )
    return (analysis_mean, solved.reshape(tile_rows, tile_cols, member_total))


def solution(mesh):
    in_specs = (
        P("gx", "gy", None),
        P(None, "gx", "gy"),
        P("gx", "gy", None),
        P("gx", "gy"),
        P("gx", "gy", None),
        P("gx", "gy", None),
    )
    out_specs = (P("gx", "gy"), P("gx", "gy", None))
    return jax.shard_map(shards, mesh=mesh, in_specs=in_specs, out_specs=out_specs, check_vma=False)
```

profile of v0, /device:TPU:1, one launch (start us, length us, event | category | flops | bytes accessed | tf_op | source)
XLA Modules:
  0.0 576.6 jit_solution(12888910316275926659)
XLA Ops:
  8.0 1.3 collective-permute-start
  9.3 5.6 collective-permute-start.1
  14.8 1.5 convert_element_type.9
  16.4 11.6 %collective-permute-start.2 = (f32[66,1,128]{2,1,0:T(1,128)S(1)}, f32[66,1,128]{2,1,0:T(1,128)S(1)}, u32[]{:S(2)}, u32[]{:S(2)}) collective-permute-start(f32[66,1,128]{2,1,0:T(1,128)S(1)} %get-tuple-element.8), channel_id=1, source_target_pairs={{1,0},{2,1},{3,2},{4,3},{5,4},{6,5},{7,6},{9,8},{10,9},{11,10},{12... | collective-permute-start | bytes 101384 | tf_op jit(solution)/shard_map/ppermute | solution.py:22
  28.0 1.9 collective-permute-start.3
  31.1 3.6 multiply_subtract_fusion.2
  34.7 1.3 collective-permute-start.4
  36.0 4.6 collective-permute-start.5
  41.7 2.9 collective-permute-start.6
  44.6 3.9 collective-permute-start.7
  49.5 3.6 multiply_subtract_fusion.1
  53.2 1.3 collective-permute-start.8
  54.5 4.6 collective-permute-start.9
  60.1 1.9 collective-permute-start.10
  62.0 5.1 collective-permute-start.11
  68.1 4.9 fusion.24
  73.1 2.2 broadcast_subtract_fusion
  77.0 1.1 gather_fusion.1
  78.4 120.3 %psum.15 = f32[128]{0:T(128)S(1)} all-reduce(f32[128]{0:T(128)S(1)} %convolution_bitcast_fusion.2), channel_id=1, replica_groups=mesh['gx'=96,'gy'=8] {'gx','gy'}, use_global_device_ids=true, to_apply=%region_4.5 | all-reduce | flops 128 | bytes 1024 | tf_op jit(solution)/shard_map/psum | solution.py:64
  198.7 337.7 %all-reduce.2.cloned.1.call-done = f32[128,128]{1,0:T(8,128)} async-done(((f32[128,128]{1,0:T(8,128)}), f32[128,128]{1,0:T(8,128)}) %all-reduce.2.cloned.1.call-update) | async-done | bytes 65552 | tf_op jit(solution)/shard_map/psum | solution.py:64
  538.2 11.7 %cholesky.16 = f32[128,128]{1,0:T(8,128)S(1)} custom-call(f32[128,128]{1,0:T(8,128)S(1)} %fusion.5), custom_call_target="Cholesky" | custom-call | tf_op jit(solution)/shard_map/jit(cholesky)/cholesky | solution.py:66
  551.2 9.8 %custom-call.13 = f32[1,128,128]{1,2,0:T(8,128)S(1)} custom-call(f32[1,128,128]{2,1,0:T(8,128)S(1)} %fusion), custom_call_target="InvertDiagBlocksLowerTriangular" | custom-call | tf_op jit(solution)/shard_map/jit(_cho_solve)/triangular_solve | solution.py:67
  561.0 2.8 convolution_convert_fusion
  564.1 5.0 fusion.28
  (47 shorter events, 11.5 us)
Async XLA Ops:
  7.2 529.2 %all-reduce.2.cloned.1.call-start = ((), (), s32[]{:S(2)}) async-start(), calls=%async_computation | async-start | bytes 131072 | tf_op jit(solution)/shard_map/psum | solution.py:64
  8.0 8.4 %collective-permute-start = (f32[1,64,128]{2,1,0:T(8,128)S(1)}, f32[1,64,128]{2,1,0:T(8,128)S(1)}, u32[]{:S(2)}, u32[]{:S(2)}) collective-permute-start(f32[1,64,128]{2,1,0:T(8,128)S(1)} %get-tuple-element.15), channel_id=1, source_target_pairs={{8,0},{16,8},{24,16},{32,24},{40,32},{48,40},{56,48},{64,56},{72,6... | collective-permute-start | bytes 98312 | tf_op jit(solution)/shard_map/ppermute | solution.py:22
  9.2 20.7 %copy-start = (f32[2,64,64]{2,1,0:T(8,128)S(1)}, f32[2,64,64]{2,1,0:T(8,128)}, u32[]{:S(2)}) copy-start(f32[2,64,64]{2,1,0:T(8,128)} %param.7) | copy-start | bytes 98308
  9.3 7.1 %collective-permute-start.1 = (f32[1,64,128]{2,1,0:T(8,128)S(1)}, f32[1,64,128]{2,1,0:T(8,128)S(1)}, u32[]{:S(2)}, u32[]{:S(2)}) collective-permute-start(f32[1,64,128]{2,1,0:T(8,128)S(1)} %get-tuple-element.14), channel_id=1, source_target_pairs={{0,8},{8,16},{16,24},{24,32},{32,40},{40,48},{48,56},{56,64},{64,7... | collective-permute-start | bytes 98312 | tf_op jit(solution)/shard_map/ppermute | solution.py:19
  16.4 13.6 %collective-permute-start.2 = (f32[66,1,128]{2,1,0:T(1,128)S(1)}, f32[66,1,128]{2,1,0:T(1,128)S(1)}, u32[]{:S(2)}, u32[]{:S(2)}) collective-permute-start(f32[66,1,128]{2,1,0:T(1,128)S(1)} %get-tuple-element.8), channel_id=1, source_target_pairs={{1,0},{2,1},{3,2},{4,3},{5,4},{6,5},{7,6},{9,8},{10,9},{11,10},{12... | collective-permute-start | bytes 101384 | tf_op jit(solution)/shard_map/ppermute | solution.py:22
  28.0 3.1 collective-permute-start.3
  31.1 9.5 %copy-start.1 = (s32[1,1,128]{2,1,0:T(1,128)S(1)}, s32[1,1,128]{2,1,0:T(1,128)}, u32[]{:S(2)}) copy-start(s32[1,1,128]{2,1,0:T(1,128)} %param.8) | copy-start | bytes 1540
  34.7 13.8 %copy-start.2 = (f32[1,1,128]{2,1,0:T(1,128)S(1)}, f32[1,1,128]{2,1,0:T(1,128)}, u32[]{:S(2)}) copy-start(f32[1,1,128]{2,1,0:T(1,128)} %param.11) | copy-start | bytes 1540
  34.7 5.9 %collective-permute-start.4 = (f32[1,64,128]{2,1,0:T(8,128)S(1)}, f32[1,64,128]{2,1,0:T(8,128)S(1)}, u32[]{:S(2)}, u32[]{:S(2)}) collective-permute-start(f32[1,64,128]{2,1,0:T(8,128)S(1)} %get-tuple-element.13), channel_id=1, source_target_pairs={{8,0},{16,8},{24,16},{32,24},{40,32},{48,40},{56,48},{64,56},{72,6... | collective-permute-start | bytes 98312 | tf_op jit(solution)/shard_map/ppermute | solution.py:22
  36.0 5.6 collective-permute-start.5
  41.7 6.9 %collective-permute-start.6 = (f32[66,1,128]{2,1,0:T(1,128)S(1)}, f32[66,1,128]{2,1,0:T(1,128)S(1)}, u32[]{:S(2)}, u32[]{:S(2)}) collective-permute-start(f32[66,1,128]{2,1,0:T(1,128)S(1)} %get-tuple-element.6), channel_id=1, source_target_pairs={{1,0},{2,1},{3,2},{4,3},{5,4},{6,5},{7,6},{9,8},{10,9},{11,10},{12... | collective-permute-start | bytes 101384 | tf_op jit(solution)/shard_map/ppermute | solution.py:22
  44.6 4.9 collective-permute-start.7
  53.2 6.5 %collective-permute-start.8 = (f32[1,64,128]{2,1,0:T(8,128)S(1)}, f32[1,64,128]{2,1,0:T(8,128)S(1)}, u32[]{:S(2)}, u32[]{:S(2)}) collective-permute-start(f32[1,64,128]{2,1,0:T(8,128)S(1)} %get-tuple-element.11), channel_id=1, source_target_pairs={{8,0},{16,8},{24,16},{32,24},{40,32},{48,40},{56,48},{64,56},{72,6... | collective-permute-start | bytes 98312 | tf_op jit(solution)/shard_map/ppermute | solution.py:22
  54.5 5.6 collective-permute-start.9
  60.1 7.0 %collective-permute-start.10 = (f32[66,1,128]{2,1,0:T(1,128)S(1)}, f32[66,1,128]{2,1,0:T(1,128)S(1)}, u32[]{:S(2)}, u32[]{:S(2)}) collective-permute-start(f32[66,1,128]{2,1,0:T(1,128)S(1)} %get-tuple-element.4), channel_id=1, source_target_pairs={{1,0},{2,1},{3,2},{4,3},{5,4},{6,5},{7,6},{9,8},{10,9},{11,10},{12... | collective-permute-start | bytes 101384 | tf_op jit(solution)/shard_map/ppermute | solution.py:22
  62.0 6.1 %collective-permute-start.11 = (f32[66,1,128]{2,1,0:T(1,128)S(1)}, f32[66,1,128]{2,1,0:T(1,128)S(1)}, u32[]{:S(2)}, u32[]{:S(2)}) collective-permute-start(f32[66,1,128]{2,1,0:T(1,128)S(1)} %get-tuple-element.5), channel_id=1, source_target_pairs={{0,1},{1,2},{2,3},{3,4},{4,5},{5,6},{6,7},{8,9},{9,10},{10,11},{11... | collective-permute-start | bytes 101384 | tf_op jit(solution)/shard_map/ppermute | solution.py:19
  73.1 5.0 copy-start.3
Sparse Core Ops, SparseCore 0:
  77.1 459.1 all-reduce.1
where the time goes:
time: 579 us; the launch traced here: 577 us
  waiting for transfers between devices  342 us (59%)
  blocking collectives  120 us (21%)
  starting transfers between devices  46 us (8%)
  other arithmetic  41.2 us (7%)
  between operations  15 us (3%)
  matrix products  9.34 us (2%)
    psum x1, waiting for transfers between devices, shards(): gram_term, cross_term = lax.psum((gram_term, cross_term), ('gx', 'gy'))  338 us
    psum x1, blocking collectives, shards(): gram_term, cross_term = lax.psum((gram_term, cross_term), ('gx', 'gy'))  120 us
    ppermute x6, starting transfers between devices, padded(): lax.ppermute(lax.slice_in_dim(block, block.shape[dim] - width, None, axis...  25.6 us
    ppermute x6, starting transfers between devices, padded(): lax.ppermute(lax.slice_in_dim(block, 0, width, axis=dim), axis, backward)  20.3 us
    another operation x3, other arithmetic, shards(): lower_factor = jnp.linalg.cholesky(gram_total)  12.4 us
  transfers between devices with their start and end apart: 13, of which 6 were waited for; matrix products, arithmetic and copies ran while one was open for 1% of the time, Pallas kernels for 0%

commit v1 on v0

v1 whole, which is shorter than its diff:
```python
import functools
import math

import jax
import jax.numpy as jnp
from jax import lax
from jax.experimental import pallas as pl
from jax.experimental.pallas import tpu as pltpu
from jax.sharding import PartitionSpec as P

M = 128
GROUPS = M // 8


def split(x):
    hi = x.astype(jnp.bfloat16)
    return hi, (x - hi.astype(jnp.float32)).astype(jnp.bfloat16)


def row_of(x, k):
    return jnp.broadcast_to(x[k : k + 1, :], x.shape)


def column_of(x, k):
    return jnp.broadcast_to(x[:, k : k + 1], (x.shape[0], 128))


def inverse_factor(gram_rows):
    sub = lax.broadcasted_iota(jnp.int32, (8, 128), 0)
    lane = lax.broadcasted_iota(jnp.int32, (8, 128), 1)
    a = [g + (lane == sub + 8 * i).astype(jnp.float32) for i, g in enumerate(gram_rows)]
    x = [(lane == sub + 8 * i).astype(jnp.float32) for i in range(GROUPS)]
    for p in range(GROUPS):
        c = [column_of(a[p], 8 * p + j) for j in range(8)]
        recip, upper, row_a, row_x = [], [], [], []
        pivots = jnp.ones((8, 128), jnp.float32)
        for k in range(8):
            pivot = row_of(c[k], k)
            r = 1.0 / pivot
            pivots = jnp.where(sub == k, pivot, pivots)
            recip.append(r)
            m = jnp.where(sub > k, c[k] * r, 0.0)
            upper.append([None] * 8)
            for j in range(k + 1, 8):
                upper[k][j] = row_of(c[j], k)
                c[j] = c[j] - m * upper[k][j]
            row_a.append(row_of(a[p], k))
            row_x.append(row_of(x[p], k))
            if k < 7:
                a[p] = a[p] - m * row_a[k]
                x[p] = x[p] - m * row_x[k]
        for i in range(p + 1, GROUPS):
            e = [column_of(a[i], 8 * p + j) for j in range(8)]
            for k in range(8):
                m = e[k] * recip[k]
                for j in range(k + 1, 8):
                    e[j] = e[j] - m * upper[k][j]
                a[i] = a[i] - m * row_a[k]
                x[i] = x[i] - m * row_x[k]
        x[p] = x[p] * lax.rsqrt(pivots)
    return x


def transform_kernel(rows, gram_ref, anom_hbm, mean_ref, out_mean, out_hbm, anom, out, mix, flat, sem_in, sem_out):
    chunks = 4
    cells = anom.shape[0] // chunks
    load = pltpu.make_async_copy(anom_hbm, anom, sem_in)
    load.start()
    groups = []
    for i in range(GROUPS):
        piece, start = divmod(8 * i, rows)
        groups.append(gram_ref[piece, start : start + 8, :])
    x = inverse_factor(groups)
    cross = jnp.broadcast_to(gram_ref[0, rows : rows + 1, :], (8, 128))
    total = jnp.zeros((8, 128), jnp.float32)
    for i in range(GROUPS):
        y = jnp.sum(x[i] * cross, axis=1, keepdims=True)
        total = total + x[i] * y
    weights = jnp.broadcast_to(jnp.sum(total, axis=0, keepdims=True), (16, 128))
    for i in range(0, GROUPS, 2):
        hi, lo = split(jnp.concatenate([x[i], x[i + 1]], axis=0))
        mix[8 * i : 8 * i + 16, 0:128] = hi
        mix[8 * i : 8 * i + 16, 128:256] = hi
        mix[128 + 8 * i : 128 + 8 * i + 16, 0:128] = lo
        mix[128 + 8 * i : 128 + 8 * i + 16, 128:256] = jnp.zeros((16, 128), jnp.bfloat16)
    w_hi, w_lo = split(weights)
    w_both = jnp.concatenate([w_hi, w_hi], axis=1)
    w_low = jnp.concatenate([w_lo, jnp.zeros_like(w_lo)], axis=1)
    w_rows = jnp.concatenate([w_both, w_low], axis=0)
    load.wait()
    nt = (((1,), (1,)), ((), ()))
    for q in range(chunks):
        part = pl.ds(q * cells, cells)
        block = anom[part, :]
        both = lax.dot_general(block, mix[...], nt, preferred_element_type=jnp.float32)
        out[part, :] = (both[:, 0:128] + both[:, 128:256]).astype(jnp.bfloat16)
        pltpu.make_async_copy(out.at[part], out_hbm.at[part], sem_out.at[q]).start()
    for q in range(chunks):
        part = pl.ds(q * cells, cells)
        shift = lax.dot_general(w_rows, anom[part, :], nt, preferred_element_type=jnp.float32)
        line = shift[0:1, :] + shift[16:17, :]
        for i in range(cells // 128):
            n = q * (cells // 128) + i
            flat[n : n + 1, :] = line[:, 128 * i : 128 * i + 128]
    lines = flat[...]
    ny = out_mean.shape[1]
    half = flat.shape[0]
    even = lines[:, 0:ny]
    odd = pltpu.roll(lines, 128 - ny, axis=1)[:, 0:ny]
    out_mean[pl.ds(0, half, stride=2), :] = mean_ref[pl.ds(0, half, stride=2), :] + even
    out_mean[pl.ds(1, half, stride=2), :] = mean_ref[pl.ds(1, half, stride=2), :] + odd
    for q in range(chunks):
        part = pl.ds(q * cells, cells)
        pltpu.make_async_copy(out.at[part], out_hbm.at[part], sem_out.at[q]).wait()


def transform(gram, anom, mean):
    pieces, piece_rows, _ = gram.shape
    cells = anom.shape[0]
    return pl.pallas_call(
        functools.partial(transform_kernel, piece_rows - 1),
        out_shape=(
            jax.ShapeDtypeStruct(mean.shape, jnp.float32),
            jax.ShapeDtypeStruct((cells, M), jnp.bfloat16),
        ),
        in_specs=[
            pl.BlockSpec(memory_space=pltpu.VMEM),
            pl.BlockSpec(memory_space=pl.ANY),
            pl.BlockSpec(memory_space=pltpu.VMEM),
        ],
        out_specs=(pl.BlockSpec(memory_space=pltpu.VMEM), pl.BlockSpec(memory_space=pl.ANY)),
        scratch_shapes=[
            pltpu.VMEM((cells, 2 * M), jnp.bfloat16),
            pltpu.VMEM((cells, M), jnp.bfloat16),
            pltpu.VMEM((2 * M, 2 * M), jnp.bfloat16),
            pltpu.VMEM((cells // 128, 128), jnp.float32),
            pltpu.SemaphoreType.DMA,
            pltpu.SemaphoreType.DMA((4,)),
        ],
        compiler_params=pltpu.CompilerParams(vmem_limit_bytes=24 * 2**20),
    )(gram, anom, mean)


STEPS = 3
SIDE = 64
PITCH = 80
EDGE = 8
DIFFUSION = 0.2
HIGHEST = lax.Precision.HIGHEST
MESH = pl.DeviceIdType.MESH


def forecast_kernel(
    nz, total_slots,
    members_hbm, courant_ref, cells_ref, count_ref, value_ref, weight_ref,
    gram_out, anom_hbm, mean_out,
    members, state0, state1, state2, state3, along, across, column_out, column_in,
    observed, anom, parts, from_gy, held_y, from_y, held_z, from_z, held_gy, whole,
    sem_members, sem_anom, halo_send, halo_recv, gy_send, gy_recv, y_send, y_recv, z_send, z_recv, back_send, back_recv,
):
    states = [state0, state1, state2, state3]
    gx, gy = lax.axis_index("gx"), lax.axis_index("gy")
    n_gx, n_gy = lax.axis_size("gx"), lax.axis_size("gy")
    ny = n_gx // nz
    y, z = gx // nz, lax.rem(gx, nz)
    has_west, has_east, has_south, has_north = gx > 0, gx < n_gx - 1, gy > 0, gy < n_gy - 1

    load = pltpu.make_async_copy(members_hbm, members, sem_members)
    load.start()

    barrier = pltpu.get_barrier_semaphore()

    def greet(count, peer_of):
        def body(i, carry):
            pl.semaphore_signal(barrier, inc=1, device_id=peer_of(i), device_id_type=MESH)
            return carry
        lax.fori_loop(1, count, body, 0)

    def gy_peer(i):
        return lax.rem(gy + i, n_gy)

    def y_peer(i):
        return lax.rem(y + i, ny)

    def z_peer(i):
        return lax.rem(z + i, nz)

    greet(n_gy, lambda i: (gx, gy_peer(i)))
    greet(ny, lambda i: (y_peer(i) * nz + z, gy))
    greet(nz, lambda i: (y * nz + z_peer(i), gy))
    far_west = jnp.logical_and(has_west, z == 0)
    far_east = jnp.logical_and(has_east, z == nz - 1)

    @pl.when(far_west)
    def _():
        pl.semaphore_signal(barrier, inc=1, device_id=(gx - 1, gy), device_id_type=MESH)

    @pl.when(far_east)
    def _():
        pl.semaphore_signal(barrier, inc=1, device_id=(gx + 1, gy), device_id_type=MESH)

    zeros = jnp.zeros((SIDE, 128), jnp.float32)
    low_row, high_row = pl.ds(EDGE, SIDE), pl.ds((SIDE + 1) * PITCH + EDGE, SIDE)
    first_row, last_row = pl.ds(PITCH + EDGE, SIDE), pl.ds(SIDE * PITCH + EDGE, SIDE)

    def column(cell, shift=0):
        return pl.ds((1 + shift) * PITCH + EDGE + cell, SIDE, stride=PITCH)

    for step in range(STEPS):
        @pl.when(jnp.logical_not(has_west))
        def _():
            states[step][low_row, :] = zeros

        @pl.when(jnp.logical_not(has_east))
        def _():
            states[step][high_row, :] = zeros

        @pl.when(jnp.logical_not(has_south))
        def _():
            column_in[step, 0] = zeros

        @pl.when(jnp.logical_not(has_north))
        def _():
            column_in[step, 1] = zeros

    load.wait()

    def fill(i, carry):
        state0[pl.ds(pl.multiple_of((i + 1) * PITCH + EDGE, 8), SIDE), :] = members[
            pl.ds(pl.multiple_of(i * SIDE, SIDE), SIDE), :
        ].astype(jnp.float32)
        return carry

    lax.fori_loop(0, SIDE, fill, 0)
    column_out[0, 0] = state0[column(0), :]
    column_out[0, 1] = state0[column(SIDE - 1), :]

    pl.semaphore_wait(
        barrier,
        (n_gy - 1) + (ny - 1) + (nz - 1) + far_west.astype(jnp.int32) + far_east.astype(jnp.int32),
    )

    def halo_copies(step):
        state = states[step]
        west = pltpu.make_async_remote_copy(
            src_ref=state.at[first_row], dst_ref=state.at[high_row],
            send_sem=halo_send.at[step, 0], recv_sem=halo_recv.at[step, 1],
            device_id=(gx - 1, gy), device_id_type=MESH,
        )
        east = pltpu.make_async_remote_copy(
            src_ref=state.at[last_row], dst_ref=state.at[low_row],
            send_sem=halo_send.at[step, 1], recv_sem=halo_recv.at[step, 0],
            device_id=(gx + 1, gy), device_id_type=MESH,
        )
        south = pltpu.make_async_remote_copy(
            src_ref=column_out.at[step, 0], dst_ref=column_in.at[step, 1],
            send_sem=halo_send.at[step, 2], recv_sem=halo_recv.at[step, 3],
            device_id=(gx, gy - 1), device_id_type=MESH,
        )
        north = pltpu.make_async_remote_copy(
            src_ref=column_out.at[step, 1], dst_ref=column_in.at[step, 0],
            send_sem=halo_send.at[step, 3], recv_sem=halo_recv.at[step, 2],
            device_id=(gx, gy + 1), device_id_type=MESH,
        )
        return west, east, south, north

    def start_halo(step):
        copies = halo_copies(step)
        for there, copy in zip((has_west, has_east, has_south, has_north), copies):
            @pl.when(there)
            def _():
                copy.start()

    def finish_halo(step):
        west, east, south, north = halo_copies(step)
        for there, out, back in (
            (has_west, west, east), (has_east, east, west), (has_south, south, north), (has_north, north, south)
        ):
            @pl.when(there)
            def _():
                back.wait_recv()
                out.wait_send()

    start_halo(0)

    eye_x = lax.broadcasted_iota(jnp.int32, (SIDE, SIDE), 0)
    eye_y = lax.broadcasted_iota(jnp.int32, (SIDE, SIDE), 1)
    eye = eye_x == eye_y

    def spread(i, carry):
        rows = pl.ds(pl.multiple_of(i * SIDE, SIDE), SIDE)
        for which, target in ((0, along), (1, across)):
            line = courant_ref[which, pl.ds(i, 1), :] * (0.5 / DIFFUSION)
            tall = jnp.sum(jnp.where(eye, line, 0.0), axis=1, keepdims=True)
            target[rows, :] = jnp.broadcast_to(tall, (SIDE, 128))
        return carry

    lax.fori_loop(0, SIDE, spread, 0)

    def update(state, at, flow_at):
        centre, east, west, north, south = (state[s, :] for s in at)
        return (
            ((east + west) + (north + south) + centre)
            - along[flow_at, :] * (east - west)
            - across[flow_at, :] * (north - south)
        )

    last_scale = DIFFUSION**STEPS

    def advance_row(step, i):
        base = (i + 1) * PITCH + EDGE
        if not isinstance(base, int):
            base = pl.multiple_of(base, 8)
        shifts = (0, PITCH, -PITCH, 1, -1)
        at = [pl.ds(base + s, SIDE) for s in shifts]
        flow = i * SIDE
        if not isinstance(flow, int):
            flow = pl.multiple_of(flow, SIDE)
        out = update(states[step], at, pl.ds(flow, SIDE))
        if step == STEPS - 1:
            out = out * last_scale
        states[step + 1][at[0], :] = out

    def advance_column(step, cell, side):
        at = [column(cell), column(cell, 1), column(cell, -1), column(cell + 1), column(cell - 1)]
        column_out[step + 1, side] = update(states[step], at, pl.ds(cell, SIDE, stride=SIDE))

    for step in range(STEPS):
        finish_halo(step)
        states[step][column(-1), :] = column_in[step, 0]
        states[step][column(SIDE), :] = column_in[step, 1]
        advance_row(step, 0)
        advance_row(step, SIDE - 1)
        if step + 1 < STEPS:
            advance_column(step, 0, 0)
            advance_column(step, SIDE - 1, 1)
            start_halo(step + 1)

        def interior(i, carry, step=step):
            advance_row(step, i)
            return carry

        lax.fori_loop(1, SIDE - 1, interior, 0)

    slots = observed.shape[0]

    def pick(s, carry):
        cell = cells_ref[0, s]
        row = (cell // SIDE + 1) * PITCH + EDGE + lax.rem(cell, SIDE)
        observed[pl.ds(s, 1), :] = state3[pl.ds(row, 1), :]
        return carry

    lax.fori_loop(0, slots, pick, 0, unroll=8)

    seen = observed[...].T
    members_total = seen.shape[0]
    seen_mean = jnp.sum(seen, axis=0, keepdims=True) / members_total
    live = lax.broadcasted_iota(jnp.int32, (1, slots), 1) < count_ref[0, 0]
    weight = weight_ref[...]
    scaled = (seen - seen_mean) * jnp.where(live, weight / math.sqrt(total_slots), 0.0)
    innovation = jnp.where(live, weight * (value_ref[...] - seen_mean), 0.0)
    left = jnp.concatenate([scaled, jnp.broadcast_to(innovation, (8, slots))], axis=0)
    nt = (((1,), (1,)), ((), ()))
    gram = lax.dot_general(left, scaled, nt, precision=HIGHEST, preferred_element_type=jnp.float32)
    rows = members_total // n_gy
    for j in range(n_gy):
        parts[j, 0:rows, :] = gram[j * rows : (j + 1) * rows, :]
        parts[j, rows : rows + 1, :] = gram[members_total : members_total + 1, :]

    def exchange(count, me, peer, device, source, target, send, recv):
        def copy(i, slot):
            return pltpu.make_async_remote_copy(
                src_ref=source(peer(i)), dst_ref=target.at[slot],
                send_sem=send.at[peer(i)], recv_sem=recv.at[slot],
                device_id=device(peer(i)), device_id_type=MESH,
            )

        def begin():
            def body(i, carry):
                copy(i, me).start()
                return carry
            lax.fori_loop(1, count, body, 0)

        def end():
            def body(i, carry):
                copy(i, peer(i)).wait_recv()
                copy(i, me).wait_send()
                return carry
            lax.fori_loop(1, count, body, 0)

        return begin, end

    def total(ref, count):
        out = ref[0]
        for j in range(1, count):
            out = out + ref[j]
        return out

    gy_begin, gy_end = exchange(
        n_gy, gy, gy_peer, lambda p: (gx, p), lambda p: parts.at[p], from_gy, gy_send, gy_recv
    )
    y_begin, y_end = exchange(
        ny, y, y_peer, lambda p: (p * nz + z, gy), lambda p: held_y, from_y, y_send, y_recv
    )
    z_begin, z_end = exchange(
        nz, z, z_peer, lambda p: (y * nz + p, gy), lambda p: held_z, from_z, z_send, z_recv
    )
    back_begin, back_end = exchange(
        n_gy, gy, gy_peer, lambda p: (gx, p), lambda p: held_gy, whole, back_send, back_recv
    )

    def anomalies(i, carry):
        block = state3[pl.ds(pl.multiple_of((i + 1) * PITCH + EDGE, 8), SIDE), :]
        average = jnp.sum(block, axis=1, keepdims=True) / members_total
        hi, lo = split(block - average)
        at = pl.ds(pl.multiple_of(i * SIDE, SIDE), SIDE)
        anom[at, 0:128] = hi
        anom[at, 128:256] = lo
        mean_out[pl.ds(i, 1), :] = jnp.sum(jnp.where(eye, average, 0.0), axis=0, keepdims=True)
        return carry

    gy_begin()
    from_gy[gy] = parts[gy]
    lax.fori_loop(0, SIDE // 2, anomalies, 0)
    gy_end()
    held_y[...] = total(from_gy, n_gy)
    y_begin()
    from_y[y] = held_y[...]
    lax.fori_loop(SIDE // 2, SIDE, anomalies, 0)
    store = pltpu.make_async_copy(anom, anom_hbm, sem_anom)
    store.start()
    y_end()
    held_z[...] = total(from_y, ny)
    z_begin()
    from_z[z] = held_z[...]
    z_end()
    held_gy[...] = total(from_z, nz)
    back_begin()
    whole[gy] = held_gy[...]
    back_end()
    gram_out[...] = whole[...]
    store.wait()


def forecast(nz, n_gx, n_gy, members, courant, cells, count, value, weight):
    ny = n_gx // nz
    piece = (128 // n_gy + 1, 128)
    f32 = jnp.float32
    state = pltpu.VMEM(((SIDE + 2) * PITCH, 128), f32)
    dma = pltpu.SemaphoreType.DMA
    vmem, smem, hbm = (pl.BlockSpec(memory_space=s) for s in (pltpu.VMEM, pltpu.SMEM, pl.ANY))
    return pl.pallas_call(
        functools.partial(forecast_kernel, nz, 128 * n_gx * n_gy),
        out_shape=(
            jax.ShapeDtypeStruct((n_gy,) + piece, f32),
            jax.ShapeDtypeStruct((SIDE * SIDE, 256), jnp.bfloat16),
            jax.ShapeDtypeStruct((SIDE, SIDE), f32),
        ),
        in_specs=[hbm, vmem, smem, smem, vmem, vmem],
        out_specs=(vmem, hbm, vmem),
        scratch_shapes=[
            pltpu.VMEM((SIDE * SIDE, 128), jnp.bfloat16),
            state, state, state, state,
            pltpu.VMEM((SIDE * SIDE, 128), f32),
            pltpu.VMEM((SIDE * SIDE, 128), f32),
            pltpu.VMEM((STEPS, 2, SIDE, 128), f32),
            pltpu.VMEM((STEPS, 2, SIDE, 128), f32),
            pltpu.VMEM((128, 128), f32),
            pltpu.VMEM((SIDE * SIDE, 256), jnp.bfloat16),
            pltpu.VMEM((n_gy,) + piece, f32),
            pltpu.VMEM((n_gy,) + piece, f32),
            pltpu.VMEM(piece, f32),
            pltpu.VMEM((ny,) + piece, f32),
            pltpu.VMEM(piece, f32),
            pltpu.VMEM((nz,) + piece, f32),
            pltpu.VMEM(piece, f32),
            pltpu.VMEM((n_gy,) + piece, f32),
            dma, dma,
            dma((STEPS, 4)), dma((STEPS, 4)),
            dma((n_gy,)), dma((n_gy,)),
            dma((ny,)), dma((ny,)),
            dma((nz,)), dma((nz,)),
            dma((n_gy,)), dma((n_gy,)),
        ],
        compiler_params=pltpu.CompilerParams(
            collective_id=0, has_side_effects=True, vmem_limit_bytes=40 * 2**20
        ),
    )(members, courant, cells, count, value, weight)


def shards(nz, n_gx, n_gy, members, courant, obs_cells, obs_count, obs_value, obs_weight):
    tile_rows, tile_cols, member_total = members.shape
    flat = members.reshape(tile_rows * tile_cols, member_total)
    gram, anom, mean = forecast(
        nz, n_gx, n_gy, flat, courant,
        obs_cells.reshape(1, -1), obs_count, obs_value.reshape(1, -1), obs_weight.reshape(1, -1),
    )
    out_mean, out_anom = transform(gram, anom, mean)
    return out_mean, out_anom.reshape(members.shape)


Z_CHIPS = 12


def solution(mesh):
    n_gx, n_gy = mesh.shape["gx"], mesh.shape["gy"]
    in_specs = (
        P("gx", "gy", None),
        P(None, "gx", "gy"),
        P("gx", "gy", None),
        P("gx", "gy"),
        P("gx", "gy", None),
        P("gx", "gy", None),
    )
    out_specs = (P("gx", "gy"), P("gx", "gy", None))
    body = functools.partial(shards, Z_CHIPS, n_gx, n_gy)
    return jax.shard_map(body, mesh=mesh, in_specs=in_specs, out_specs=out_specs, check_vma=False)
```

time: 579 us -> 68.6 us (0.12)
  waiting for transfers between devices: 342 us -> 0 us
  blocking collectives: 120 us -> 0 us
  Pallas kernels: 0 us -> 63.1 us
  starting transfers between devices: 46 us -> 0 us
  other arithmetic: 41.2 us -> 0 us
  between operations: 15 us -> 1.3 us
  matrix products: 9.34 us -> 0 us
    psum x1 -> x0, waiting for transfers between devices: 338 us -> none  [shards(): gram_term, cross_term = lax.psum((gram_term, cross_term), ('gx', 'gy'))]
    psum x1 -> x0, blocking collectives: 120 us -> none  [shards(): gram_term, cross_term = lax.psum((gram_term, cross_term), ('gx', 'gy'))]
    pallas_call x0 -> x2, Pallas kernels: none -> 63.1 us  [the longest x1 56.7 us: forecast(): pl.pallas_call(functools.partial(forecast_kernel, nz, 128 * n_gx * n_gy),...]
    ppermute x12 -> x0, starting transfers between devices: 45.9 us -> none  [the longest x6 25.6 us: padded(): lax.ppermute(lax.slice_in_dim(block, block.shape[dim] - width, None, axis...]
    another operation x5 -> x0, other arithmetic: 22.9 us -> none  [the longest x3 12.4 us: shards(): lower_factor = jnp.linalg.cholesky(gram_total)]
    sub x3 -> x0, other arithmetic: 9.4 us -> none  [the longest x2 7.2 us: advance(): centre + diffusion * (east_side + west_side + north_side + south_side - 4...]
    dot_general x3 -> x0, matrix products: 6.24 us -> none  [the longest x1 5 us: shards(): jnp.dot(flat_anomaly, weights, precision=lax.Precision.HIGHEST)]
  transfers between devices with their start and end apart: 13 -> 0, of which waited for: 6 -> 0; matrix products, arithmetic and copies ran while one was open for 1% -> 0% of each run, Pallas kernels for 0% -> 0%
where the time goes in v1:
time: 68.6 us; the launch traced here: 68.4 us
  Pallas kernels  63.1 us (92%)
  local copies, waits for them, and re-layouts  4.02 us (6%)
  between operations  1.3 us (2%)
    pallas_call x1, Pallas kernels, forecast(): pl.pallas_call(functools.partial(forecast_kernel, nz, 128 * n_gx * n_gy),...  56.7 us
    pallas_call x1, Pallas kernels, transform(): pl.pallas_call(functools.partial(transform_kernel, piece_rows - 1), out_s...  6.33 us
    unnamed x10, local copies, waits for them, and re-layouts  4.02 us

profile of v1, /device:TPU:1, one launch (start us, length us, event | category | flops | bytes accessed | tf_op | source)
XLA Modules:
  0.0 68.4 jit_solution(5474570369092836227)
XLA Ops:
  1.3 0.0 copy-start
  1.3 1.2 %copy-done = bf16[64,64,128]{2,1,0:T(8,128)(2,1)S(1)} copy-done((bf16[64,64,128]{2,1,0:T(8,128)(2,1)S(1)}, bf16[64,64,128]{2,1,0:T(8,128)(2,1)}, u32[]{:S(2)}) %copy-start) | copy-done | bytes 1048600
  2.5 0.0 copy-start.1
  2.5 0.8 %copy-done.1 = f32[2,64,64]{2,1,0:T(8,128)S(1)} copy-done((f32[2,64,64]{2,1,0:T(8,128)S(1)}, f32[2,64,64]{2,1,0:T(8,128)}, u32[]{:S(2)}) %copy-start.1) | copy-done | bytes 32792
  3.3 0.0 copy-start.2
  3.3 0.7 copy-done.2
  4.0 0.0 copy-start.3
  4.0 0.7 copy-done.3
  4.7 0.0 copy-start.4
  4.7 0.7 copy-done.4
  5.3 56.7 %shard_map.77 = (f32[8,17,128]{2,1,0:T(8,128)S(1)}, bf16[4096,256]{1,0:T(8,128)(2,1)S(1)}, f32[64,64]{1,0:T(8,128)S(1)}) custom-call(bf16[4096,128]{1,0:T(8,128)(2,1)S(1)} %bitcast.5, f32[2,64,64]{2,1,0:T(8,128)S(1)} %copy-done.1, s32[1,128]{1,0:T(1,128)S(1)} %bitcast.6, s32[1,1]{1,0:T(1,128)S(6)} %copy.8.count_ref, f32[1,128]{1,0:T(1,128)S(1)} %bitcast.7, ...), custom_call_target="tpu_custom_call" | custom-call | tf_op jit(solution)/shard_map/pallas_call | solution.py:452
  62.1 6.3 %shard_map.78 = (f32[64,64]{1,0:T(8,128)}, bf16[4096,128]{1,0:T(8,128)(2,1)}) custom-call(f32[8,17,128]{2,1,0:T(8,128)S(1)} %get-tuple-element.7.gram_ref, bf16[4096,256]{1,0:T(8,128)(2,1)S(1)} %get-tuple-element.8.anom_hbm, f32[64,64]{1,0:T(8,128)S(1)} %get-tuple-element.9.mean_ref), custom_call_target="tpu_custom_call" | custom-call | tf_op jit(solution)/shard_map/pallas_call | solution.py:120
Async XLA Ops:
  1.3 1.2 %copy-start = (bf16[64,64,128]{2,1,0:T(8,128)(2,1)S(1)}, bf16[64,64,128]{2,1,0:T(8,128)(2,1)}, u32[]{:S(2)}) copy-start(bf16[64,64,128]{2,1,0:T(8,128)(2,1)} %param.6) | copy-start | bytes 3145732
  2.5 0.8 %copy-start.1 = (f32[2,64,64]{2,1,0:T(8,128)S(1)}, f32[2,64,64]{2,1,0:T(8,128)}, u32[]{:S(2)}) copy-start(f32[2,64,64]{2,1,0:T(8,128)} %courant_ref.1) | copy-start | bytes 98308
  3.3 0.7 copy-start.2
  4.0 0.7 copy-start.3
  4.7 0.7 copy-start.4

commit v2 on v1

--- a/solution.py
+++ b/solution.py
@@ -30,8 +30,12 @@
     lane = lax.broadcasted_iota(jnp.int32, (8, 128), 1)
     a = [g + (lane == sub + 8 * i).astype(jnp.float32) for i, g in enumerate(gram_rows)]
     x = [(lane == sub + 8 * i).astype(jnp.float32) for i in range(GROUPS)]
+    c = [column_of(a[0], j) for j in range(8)]
     for p in range(GROUPS):
-        c = [column_of(a[p], 8 * p + j) for j in range(8)]
+        more = p + 1 < GROUPS
+        if more:
+            e = [column_of(a[p + 1], 8 * p + j) for j in range(8)]
+            d = [column_of(a[p + 1], 8 * p + 8 + j) for j in range(8)]
         recip, upper, row_a, row_x = [], [], [], []
         pivots = jnp.ones((8, 128), jnp.float32)
         for k in range(8):
@@ -44,20 +48,31 @@
             for j in range(k + 1, 8):
                 upper[k][j] = row_of(c[j], k)
                 c[j] = c[j] - m * upper[k][j]
+            if more:
+                n = e[k] * r
+                for j in range(k + 1, 8):
+                    e[j] = e[j] - n * upper[k][j]
+                for j in range(8):
+                    d[j] = d[j] - n * row_of(e[k], j)
             row_a.append(row_of(a[p], k))
             row_x.append(row_of(x[p], k))
             if k < 7:
                 a[p] = a[p] - m * row_a[k]
                 x[p] = x[p] - m * row_x[k]
-        for i in range(p + 1, GROUPS):
-            e = [column_of(a[i], 8 * p + j) for j in range(8)]
+            if more:
+                a[p + 1] = a[p + 1] - n * row_a[k]
+                x[p + 1] = x[p + 1] - n * row_x[k]
+        for i in range(p + 2, GROUPS):
+            f = [column_of(a[i], 8 * p + j) for j in range(8)]
             for k in range(8):
-                m = e[k] * recip[k]
+                m = f[k] * recip[k]
                 for j in range(k + 1, 8):
-                    e[j] = e[j] - m * upper[k][j]
+                    f[j] = f[j] - m * upper[k][j]
                 a[i] = a[i] - m * row_a[k]
                 x[i] = x[i] - m * row_x[k]
         x[p] = x[p] * lax.rsqrt(pivots)
+        if more:
+            c = d
     return x
 
 
@@ -152,11 +167,11 @@
 
 def forecast_kernel(
     nz, total_slots,
-    members_hbm, courant_ref, cells_ref, count_ref, value_ref, weight_ref,
+    members_hbm, courant_hbm, cells_hbm, count_ref, value_hbm, weight_hbm,
     gram_out, anom_hbm, mean_out,
-    members, state0, state1, state2, state3, along, across, column_out, column_in,
+    members, courant_ref, cells_ref, value_ref, weight_ref, state0, state1, state2, state3, along, across, column_out, column_in,
     observed, anom, parts, from_gy, held_y, from_y, held_z, from_z, held_gy, whole,
-    sem_members, sem_anom, halo_send, halo_recv, gy_send, gy_recv, y_send, y_recv, z_send, z_recv, back_send, back_recv,
+    sem_members, sem_small, sem_anom, halo_send, halo_recv, gy_send, gy_recv, y_send, y_recv, z_send, z_recv, back_send, back_recv,
 ):
     states = [state0, state1, state2, state3]
     gx, gy = lax.axis_index("gx"), lax.axis_index("gy")
@@ -167,6 +182,19 @@
 
     load = pltpu.make_async_copy(members_hbm, members, sem_members)
     load.start()
+    smalls = [
+        pltpu.make_async_copy(source, target, sem_small.at[i])
+        for i, (source, target) in enumerate(
+            (
+                (courant_hbm, courant_ref),
+                (cells_hbm, cells_ref),
+                (value_hbm, value_ref),
+                (weight_hbm, weight_ref),
+            )
+        )
+    ]
+    for small in smalls:
+        small.start()
 
     barrier = pltpu.get_barrier_semaphore()
 
@@ -231,7 +259,7 @@
         ].astype(jnp.float32)
         return carry
 
-    lax.fori_loop(0, SIDE, fill, 0)
+    lax.fori_loop(0, SIDE, fill, 0, unroll=4)
     column_out[0, 0] = state0[column(0), :]
     column_out[0, 1] = state0[column(SIDE - 1), :]
 
@@ -282,6 +310,7 @@
                 out.wait_send()
 
     start_halo(0)
+    smalls[0].wait()
 
     eye_x = lax.broadcasted_iota(jnp.int32, (SIDE, SIDE), 0)
     eye_y = lax.broadcasted_iota(jnp.int32, (SIDE, SIDE), 1)
@@ -295,7 +324,7 @@
             target[rows, :] = jnp.broadcast_to(tall, (SIDE, 128))
         return carry
 
-    lax.fori_loop(0, SIDE, spread, 0)
+    lax.fori_loop(0, SIDE, spread, 0, unroll=8)
 
     def update(state, at, flow_at):
         centre, east, west, north, south = (state[s, :] for s in at)
@@ -340,7 +369,7 @@
             advance_row(step, i)
             return carry
 
-        lax.fori_loop(1, SIDE - 1, interior, 0)
+        lax.fori_loop(1, SIDE - 1, interior, 0, unroll=2)
 
     slots = observed.shape[0]
 
@@ -350,6 +379,8 @@
         observed[pl.ds(s, 1), :] = state3[pl.ds(row, 1), :]
         return carry
 
+    for small in smalls[1:]:
+        small.wait()
     lax.fori_loop(0, slots, pick, 0, unroll=8)
 
     seen = observed[...].T
@@ -421,12 +452,12 @@
 
     gy_begin()
     from_gy[gy] = parts[gy]
-    lax.fori_loop(0, SIDE // 2, anomalies, 0)
+    lax.fori_loop(0, SIDE // 2, anomalies, 0, unroll=8)
     gy_end()
     held_y[...] = total(from_gy, n_gy)
     y_begin()
     from_y[y] = held_y[...]
-    lax.fori_loop(SIDE // 2, SIDE, anomalies, 0)
+    lax.fori_loop(SIDE // 2, SIDE, anomalies, 0, unroll=8)
     store = pltpu.make_async_copy(anom, anom_hbm, sem_anom)
     store.start()
     y_end()
@@ -442,13 +473,19 @@
     store.wait()
 
 
+def keep(array):
+    return pltpu.with_memory_space_constraint(array, pltpu.HBM)
+
+
 def forecast(nz, n_gx, n_gy, members, courant, cells, count, value, weight):
     ny = n_gx // nz
     piece = (128 // n_gy + 1, 128)
     f32 = jnp.float32
     state = pltpu.VMEM(((SIDE + 2) * PITCH, 128), f32)
     dma = pltpu.SemaphoreType.DMA
-    vmem, smem, hbm = (pl.BlockSpec(memory_space=s) for s in (pltpu.VMEM, pltpu.SMEM, pl.ANY))
+    vmem, smem, hbm, far = (
+        pl.BlockSpec(memory_space=s) for s in (pltpu.VMEM, pltpu.SMEM, pl.ANY, pltpu.HBM)
+    )
     return pl.pallas_call(
         functools.partial(forecast_kernel, nz, 128 * n_gx * n_gy),
         out_shape=(
@@ -456,10 +493,14 @@
             jax.ShapeDtypeStruct((SIDE * SIDE, 256), jnp.bfloat16),
             jax.ShapeDtypeStruct((SIDE, SIDE), f32),
         ),
-        in_specs=[hbm, vmem, smem, smem, vmem, vmem],
+        in_specs=[far, far, far, smem, far, far],
         out_specs=(vmem, hbm, vmem),
         scratch_shapes=[
             pltpu.VMEM((SIDE * SIDE, 128), jnp.bfloat16),
+            pltpu.VMEM((2, SIDE, SIDE), f32),
+            pltpu.SMEM((1, 128), jnp.int32),
+            pltpu.VMEM((1, 128), f32),
+            pltpu.VMEM((1, 128), f32),
             state, state, state, state,
             pltpu.VMEM((SIDE * SIDE, 128), f32),
             pltpu.VMEM((SIDE * SIDE, 128), f32),
@@ -475,7 +516,7 @@
             pltpu.VMEM((nz,) + piece, f32),
             pltpu.VMEM(piece, f32),
             pltpu.VMEM((n_gy,) + piece, f32),
-            dma, dma,
+            dma, dma((4,)), dma,
             dma((STEPS, 4)), dma((STEPS, 4)),
             dma((n_gy,)), dma((n_gy,)),
             dma((ny,)), dma((ny,)),
@@ -485,7 +526,7 @@
         compiler_params=pltpu.CompilerParams(
             collective_id=0, has_side_effects=True, vmem_limit_bytes=40 * 2**20
         ),
-    )(members, courant, cells, count, value, weight)
+    )(keep(members), keep(courant), keep(cells), count, keep(value), keep(weight))
 
 
 def shards(nz, n_gx, n_gy, members, courant, obs_cells, obs_count, obs_value, obs_weight):

time: 68.6 us -> 61.1 us (0.89)
  local copies, waits for them, and re-layouts: 4.02 us -> 0 us
  Pallas kernels: 63.1 us -> 59.7 us
    unnamed x10 -> x0, local copies, waits for them, and re-layouts: 4.02 us -> none
    pallas_call x1, Pallas kernels: 56.7 us -> 54 us  [forecast(): pl.pallas_call(functools.partial(forecast_kernel, nz, 128 * n_gx * n_gy),...]
where the time goes in v2:
time: 61.1 us; the launch traced here: 61 us
  Pallas kernels  59.7 us (98%)
  between operations  1.28 us (2%)
    pallas_call x1, Pallas kernels, forecast(): pl.pallas_call(functools.partial(forecast_kernel, nz, 128 * n_gx * n_gy),...  54 us
    pallas_call x1, Pallas kernels, transform(): pl.pallas_call(functools.partial(transform_kernel, piece_rows - 1), out_s...  5.68 us

profile of v2, /device:TPU:1, one launch (start us, length us, event | category | flops | bytes accessed | tf_op | source)
XLA Modules:
  0.0 61.0 jit_solution(2298256299504118913)
XLA Ops:
  1.3 54.0 %shard_map.77 = (f32[8,17,128]{2,1,0:T(8,128)S(1)}, bf16[4096,256]{1,0:T(8,128)(2,1)S(1)}, f32[64,64]{1,0:T(8,128)S(1)}) custom-call(bf16[4096,128]{1,0:T(8,128)(2,1)} %bitcast.5, f32[2,64,64]{2,1,0:T(8,128)} %courant_hbm.1, s32[1,128]{1,0:T(1,128)} %bitcast.6, s32[1,1]{1,0:T(1,128)S(6)} %copy.8.count_ref, f32[1,128]{1,0:T(1,128)} %bitcast.7, f32[1,128]{1,0:T(1,128)} %bitcast.8), custom_call_target="tpu_custom_call" | custom-call | tf_op jit(solution)/shard_map/pallas_call | solution.py:489
  55.3 5.7 %shard_map.78 = (f32[64,64]{1,0:T(8,128)}, bf16[4096,128]{1,0:T(8,128)(2,1)}) custom-call(f32[8,17,128]{2,1,0:T(8,128)S(1)} %get-tuple-element.7.gram_ref, bf16[4096,256]{1,0:T(8,128)(2,1)S(1)} %get-tuple-element.8.anom_hbm, f32[64,64]{1,0:T(8,128)S(1)} %get-tuple-element.9.mean_ref), custom_call_target="tpu_custom_call" | custom-call | tf_op jit(solution)/shard_map/pallas_call | solution.py:135

commit v3 on v2

--- a/solution.py
+++ b/solution.py
@@ -171,7 +171,7 @@
     gram_out, anom_hbm, mean_out,
     members, courant_ref, cells_ref, value_ref, weight_ref, state0, state1, state2, state3, along, across, column_out, column_in,
     observed, anom, parts, from_gy, held_y, from_y, held_z, from_z, held_gy, whole,
-    sem_members, sem_small, sem_anom, halo_send, halo_recv, gy_send, gy_recv, y_send, y_recv, z_send, z_recv, back_send, back_recv,
+    known, sem_members, sem_small, sem_anom, halo_send, halo_recv, gy_send, gy_recv, y_send, y_recv, z_send, z_recv, back_send, back_recv,
 ):
     states = [state0, state1, state2, state3]
     gx, gy = lax.axis_index("gx"), lax.axis_index("gy")
@@ -213,9 +213,14 @@
     def z_peer(i):
         return lax.rem(z + i, nz)
 
+    def greet_ring(semaphore, distance, along_y):
+        for shift in (distance, (ny if along_y else nz) - distance):
+            target = y_peer(shift) * nz + z if along_y else y * nz + z_peer(shift)
+            pl.semaphore_signal(semaphore, inc=1, device_id=(target, gy), device_id_type=MESH)
+
     greet(n_gy, lambda i: (gx, gy_peer(i)))
-    greet(ny, lambda i: (y_peer(i) * nz + z, gy))
-    greet(nz, lambda i: (y * nz + z_peer(i), gy))
+    greet_ring(barrier, 1, True)
+    greet_ring(barrier, 1, False)
     far_west = jnp.logical_and(has_west, z == 0)
     far_east = jnp.logical_and(has_east, z == nz - 1)
 
@@ -253,63 +258,56 @@
 
     load.wait()
 
+    def rows_at(start, unit):
+        return pl.ds(start if isinstance(start, int) else pl.multiple_of(start, unit), SIDE)
+
     def fill(i, carry):
-        state0[pl.ds(pl.multiple_of((i + 1) * PITCH + EDGE, 8), SIDE), :] = members[
-            pl.ds(pl.multiple_of(i * SIDE, SIDE), SIDE), :
-        ].astype(jnp.float32)
+        state0[rows_at((i + 1) * PITCH + EDGE, 8), :] = members[rows_at(i * SIDE, SIDE), :].astype(jnp.float32)
         return carry
 
-    lax.fori_loop(0, SIDE, fill, 0, unroll=4)
+    fill(0, 0)
+    fill(SIDE - 1, 0)
+
+    pl.semaphore_wait(
+        barrier,
+        (n_gy - 1) + 4 + far_west.astype(jnp.int32) + far_east.astype(jnp.int32),
+    )
+
+    there = (has_west, has_east, has_south, has_north)
+    halo_devices = ((gx - 1, gy), (gx + 1, gy), (gx, gy - 1), (gx, gy + 1))
+
+    def halo_copy(step, side):
+        if side < 2:
+            source = states[step].at[(first_row, last_row)[side]]
+            target = states[step].at[(high_row, low_row)[side]]
+        else:
+            source, target = column_out.at[step, side - 2], column_in.at[step, 3 - side]
+        return pltpu.make_async_remote_copy(
+            src_ref=source, dst_ref=target,
+            send_sem=halo_send.at[step, side], recv_sem=halo_recv.at[step, side ^ 1],
+            device_id=halo_devices[side], device_id_type=MESH,
+        )
+
+    def start_halo(step, sides):
+        for side in sides:
+            @pl.when(there[side])
+            def _():
+                halo_copy(step, side).start()
+
+    def finish_halo(step):
+        for side in range(4):
+            @pl.when(there[side])
+            def _():
+                halo_copy(step, side ^ 1).wait_recv()
+                halo_copy(step, side).wait_send()
+
+    start_halo(0, (0, 1))
+    greet_ring(known.at[0], 1, True)
+    greet_ring(known.at[1], 1, False)
+    lax.fori_loop(1, SIDE - 1, fill, 0, unroll=2)
     column_out[0, 0] = state0[column(0), :]
     column_out[0, 1] = state0[column(SIDE - 1), :]
-
-    pl.semaphore_wait(
-        barrier,
-        (n_gy - 1) + (ny - 1) + (nz - 1) + far_west.astype(jnp.int32) + far_east.astype(jnp.int32),
-    )
-
-    def halo_copies(step):
-        state = states[step]
-        west = pltpu.make_async_remote_copy(
-            src_ref=state.at[first_row], dst_ref=state.at[high_row],
-            send_sem=halo_send.at[step, 0], recv_sem=halo_recv.at[step, 1],
-            device_id=(gx - 1, gy), device_id_type=MESH,
-        )
-        east = pltpu.make_async_remote_copy(
-            src_ref=state.at[last_row], dst_ref=state.at[low_row],
-            send_sem=halo_send.at[step, 1], recv_sem=halo_recv.at[step, 0],
-            device_id=(gx + 1, gy), device_id_type=MESH,
-        )
-        south = pltpu.make_async_remote_copy(
-            src_ref=column_out.at[step, 0], dst_ref=column_in.at[step, 1],
-            send_sem=halo_send.at[step, 2], recv_sem=halo_recv.at[step, 3],
-            device_id=(gx, gy - 1), device_id_type=MESH,
-        )
-        north = pltpu.make_async_remote_copy(
-            src_ref=column_out.at[step, 1], dst_ref=column_in.at[step, 0],
-            send_sem=halo_send.at[step, 3], recv_sem=halo_recv.at[step, 2],
-            device_id=(gx, gy + 1), device_id_type=MESH,
-        )
-        return west, east, south, north
-
-    def start_halo(step):
-        copies = halo_copies(step)
-        for there, copy in zip((has_west, has_east, has_south, has_north), copies):
-            @pl.when(there)
-            def _():
-                copy.start()
-
-    def finish_halo(step):
-        west, east, south, north = halo_copies(step)
-        for there, out, back in (
-            (has_west, west, east), (has_east, east, west), (has_south, south, north), (has_north, north, south)
-        ):
-            @pl.when(there)
-            def _():
-                back.wait_recv()
-                out.wait_send()
-
-    start_halo(0)
+    start_halo(0, (2, 3))
     smalls[0].wait()
 
     eye_x = lax.broadcasted_iota(jnp.int32, (SIDE, SIDE), 0)
@@ -337,39 +335,56 @@
     last_scale = DIFFUSION**STEPS
 
     def advance_row(step, i):
-        base = (i + 1) * PITCH + EDGE
-        if not isinstance(base, int):
-            base = pl.multiple_of(base, 8)
-        shifts = (0, PITCH, -PITCH, 1, -1)
-        at = [pl.ds(base + s, SIDE) for s in shifts]
-        flow = i * SIDE
-        if not isinstance(flow, int):
-            flow = pl.multiple_of(flow, SIDE)
-        out = update(states[step], at, pl.ds(flow, SIDE))
+        base = rows_at((i + 1) * PITCH + EDGE, 8).start
+        at = [pl.ds(base + s, SIDE) for s in (0, PITCH, -PITCH, 1, -1)]
+        out = update(states[step], at, rows_at(i * SIDE, SIDE))
         if step == STEPS - 1:
             out = out * last_scale
         states[step + 1][at[0], :] = out
 
-    def advance_column(step, cell, side):
+    def advance_column(step, cell):
         at = [column(cell), column(cell, 1), column(cell, -1), column(cell + 1), column(cell - 1)]
-        column_out[step + 1, side] = update(states[step], at, pl.ds(cell, SIDE, stride=SIDE))
-
-    for step in range(STEPS):
-        finish_halo(step)
+        return update(states[step], at, pl.ds(cell, SIDE, stride=SIDE))
+
+    def place_columns(step):
         states[step][column(-1), :] = column_in[step, 0]
         states[step][column(SIDE), :] = column_in[step, 1]
+
+    def advance_ends(step):
+        place_columns(step)
         advance_row(step, 0)
         advance_row(step, SIDE - 1)
-        if step + 1 < STEPS:
-            advance_column(step, 0, 0)
-            advance_column(step, SIDE - 1, 1)
-            start_halo(step + 1)
-
-        def interior(i, carry, step=step):
+
+    def interior(step):
+        def body(i, carry):
             advance_row(step, i)
             return carry
-
-        lax.fori_loop(1, SIDE - 1, interior, 0, unroll=2)
+        lax.fori_loop(1, SIDE - 1, body, 0, unroll=2)
+
+    for step in range(STEPS - 1):
+        finish_halo(step)
+        advance_ends(step)
+        start_halo(step + 1, (0, 1))
+        column_out[step + 1, 0] = advance_column(step, 0)
+        column_out[step + 1, 1] = advance_column(step, SIDE - 1)
+        start_halo(step + 1, (2, 3))
+        if step == 0:
+            pl.semaphore_wait(known.at[0], 2)
+            pl.semaphore_wait(known.at[1], 2)
+            greet_ring(known.at[2], 2, True)
+            greet_ring(known.at[3], 2, False)
+        if step == 1:
+            pl.semaphore_wait(known.at[2], 2)
+            pl.semaphore_wait(known.at[3], 2)
+            greet_ring(known.at[4], 2, False)
+        interior(step)
+
+    final = STEPS - 1
+    interior(final)
+    finish_halo(final)
+    advance_ends(final)
+    for cell in (0, SIDE - 1):
+        states[STEPS][column(cell), :] = advance_column(final, cell) * last_scale
 
     slots = observed.shape[0]
 
@@ -381,7 +396,7 @@
 
     for small in smalls[1:]:
         small.wait()
-    lax.fori_loop(0, slots, pick, 0, unroll=8)
+    lax.fori_loop(0, slots, pick, 0, unroll=16)
 
     seen = observed[...].T
     members_total = seen.shape[0]
@@ -462,6 +477,7 @@
     store.start()
     y_end()
     held_z[...] = total(from_y, ny)
+    pl.semaphore_wait(known.at[4], 2)
     z_begin()
     from_z[z] = held_z[...]
     z_end()
@@ -516,6 +532,7 @@
             pltpu.VMEM((nz,) + piece, f32),
             pltpu.VMEM(piece, f32),
             pltpu.VMEM((n_gy,) + piece, f32),
+            pltpu.SemaphoreType.REGULAR((5,)),
             dma, dma((4,)), dma,
             dma((STEPS, 4)), dma((STEPS, 4)),
             dma((n_gy,)), dma((n_gy,)),

time: 61.1 us -> 57.6 us (0.943)
  Pallas kernels: 59.7 us -> 56.1 us
    pallas_call x1, Pallas kernels: 54 us -> 50.5 us  [forecast(): pl.pallas_call(functools.partial(forecast_kernel, nz, 128 * n_gx * n_gy),...]
where the time goes in v3:
time: 57.6 us; the launch traced here: 57.4 us
  Pallas kernels  56.1 us (97%)
  between operations  1.28 us (2%)
    pallas_call x1, Pallas kernels, forecast(): pl.pallas_call(functools.partial(forecast_kernel, nz, 128 * n_gx * n_gy),...  50.5 us
    pallas_call x1, Pallas kernels, transform(): pl.pallas_call(functools.partial(transform_kernel, piece_rows - 1), out_s...  5.69 us

profile of v3, /device:TPU:1, one launch (start us, length us, event | category | flops | bytes accessed | tf_op | source)
XLA Modules:
  0.0 57.4 jit_solution(11403640085211605175)
XLA Ops:
  1.3 50.5 %shard_map.77 = (f32[8,17,128]{2,1,0:T(8,128)S(1)}, bf16[4096,256]{1,0:T(8,128)(2,1)S(1)}, f32[64,64]{1,0:T(8,128)S(1)}) custom-call(bf16[4096,128]{1,0:T(8,128)(2,1)} %bitcast.5, f32[2,64,64]{2,1,0:T(8,128)} %courant_hbm.1, s32[1,128]{1,0:T(1,128)} %bitcast.6, s32[1,1]{1,0:T(1,128)S(6)} %copy.8.count_ref, f32[1,128]{1,0:T(1,128)} %bitcast.7, f32[1,128]{1,0:T(1,128)} %bitcast.8), custom_call_target="tpu_custom_call" | custom-call | tf_op jit(solution)/shard_map/pallas_call | solution.py:505
  51.7 5.7 %shard_map.78 = (f32[64,64]{1,0:T(8,128)}, bf16[4096,128]{1,0:T(8,128)(2,1)}) custom-call(f32[8,17,128]{2,1,0:T(8,128)S(1)} %get-tuple-element.7.gram_ref, bf16[4096,256]{1,0:T(8,128)(2,1)S(1)} %get-tuple-element.8.anom_hbm, f32[64,64]{1,0:T(8,128)S(1)} %get-tuple-element.9.mean_ref), custom_call_target="tpu_custom_call" | custom-call | tf_op jit(solution)/shard_map/pallas_call | solution.py:135

commit v4 on v3

--- a/solution.py
+++ b/solution.py
@@ -198,12 +198,6 @@
 
     barrier = pltpu.get_barrier_semaphore()
 
-    def greet(count, peer_of):
-        def body(i, carry):
-            pl.semaphore_signal(barrier, inc=1, device_id=peer_of(i), device_id_type=MESH)
-            return carry
-        lax.fori_loop(1, count, body, 0)
-
     def gy_peer(i):
         return lax.rem(gy + i, n_gy)
 
@@ -213,14 +207,19 @@
     def z_peer(i):
         return lax.rem(z + i, nz)
 
-    def greet_ring(semaphore, distance, along_y):
-        for shift in (distance, (ny if along_y else nz) - distance):
-            target = y_peer(shift) * nz + z if along_y else y * nz + z_peer(shift)
-            pl.semaphore_signal(semaphore, inc=1, device_id=(target, gy), device_id_type=MESH)
-
-    greet(n_gy, lambda i: (gx, gy_peer(i)))
-    greet_ring(barrier, 1, True)
-    greet_ring(barrier, 1, False)
+    rings = {
+        "gy": (n_gy, lambda i: (gx, gy_peer(i))),
+        "y": (ny, lambda i: (y_peer(i) * nz + z, gy)),
+        "z": (nz, lambda i: (y * nz + z_peer(i), gy)),
+    }
+
+    def greet_ring(ring, semaphore, distance):
+        count, device = rings[ring]
+        for shift in (distance, count - distance):
+            pl.semaphore_signal(semaphore, inc=1, device_id=device(shift), device_id_type=MESH)
+
+    for ring in rings:
+        greet_ring(ring, barrier, 1)
     far_west = jnp.logical_and(has_west, z == 0)
     far_east = jnp.logical_and(has_east, z == nz - 1)
 
@@ -270,7 +269,7 @@
 
     pl.semaphore_wait(
         barrier,
-        (n_gy - 1) + 4 + far_west.astype(jnp.int32) + far_east.astype(jnp.int32),
+        6 + far_west.astype(jnp.int32) + far_east.astype(jnp.int32),
     )
 
     there = (has_west, has_east, has_south, has_north)
@@ -302,8 +301,8 @@
                 halo_copy(step, side).wait_send()
 
     start_halo(0, (0, 1))
-    greet_ring(known.at[0], 1, True)
-    greet_ring(known.at[1], 1, False)
+    for i, ring in enumerate(rings):
+        greet_ring(ring, known.at[0, i], 1)
     lax.fori_loop(1, SIDE - 1, fill, 0, unroll=2)
     column_out[0, 0] = state0[column(0), :]
     column_out[0, 1] = state0[column(SIDE - 1), :]
@@ -369,14 +368,13 @@
         column_out[step + 1, 1] = advance_column(step, SIDE - 1)
         start_halo(step + 1, (2, 3))
         if step == 0:
-            pl.semaphore_wait(known.at[0], 2)
-            pl.semaphore_wait(known.at[1], 2)
-            greet_ring(known.at[2], 2, True)
-            greet_ring(known.at[3], 2, False)
+            for i, ring in enumerate(rings):
+                pl.semaphore_wait(known.at[0, i], 2)
+                greet_ring(ring, known.at[1, i], 2)
         if step == 1:
-            pl.semaphore_wait(known.at[2], 2)
-            pl.semaphore_wait(known.at[3], 2)
-            greet_ring(known.at[4], 2, False)
+            for i in range(len(rings)):
+                pl.semaphore_wait(known.at[1, i], 2)
+            greet_ring("z", known.at[2, 2], 2)
         interior(step)
 
     final = STEPS - 1
@@ -423,9 +421,10 @@
 
         def begin():
             def body(i, carry):
-                copy(i, me).start()
+                half = (i + 1) // 2
+                copy(count // 2 + half * (1 - 2 * lax.rem(i, 2)), me).start()
                 return carry
-            lax.fori_loop(1, count, body, 0)
+            lax.fori_loop(0, count - 1, body, 0)
 
         def end():
             def body(i, carry):
@@ -477,7 +476,7 @@
     store.start()
     y_end()
     held_z[...] = total(from_y, ny)
-    pl.semaphore_wait(known.at[4], 2)
+    pl.semaphore_wait(known.at[2, 2], 2)
     z_begin()
     from_z[z] = held_z[...]
     z_end()
@@ -532,7 +531,7 @@
             pltpu.VMEM((nz,) + piece, f32),
             pltpu.VMEM(piece, f32),
             pltpu.VMEM((n_gy,) + piece, f32),
-            pltpu.SemaphoreType.REGULAR((5,)),
+            pltpu.SemaphoreType.REGULAR((3, 3)),
             dma, dma((4,)), dma,
             dma((STEPS, 4)), dma((STEPS, 4)),
             dma((n_gy,)), dma((n_gy,)),

time: 57.6 us -> 56.4 us (0.979)
  Pallas kernels: 56.1 us -> 54.9 us
    pallas_call x1, Pallas kernels: 50.5 us -> 49.2 us  [forecast(): pl.pallas_call(functools.partial(forecast_kernel, nz, 128 * n_gx * n_gy),...]
where the time goes in v4:
time: 56.4 us; the launch traced here: 56.2 us
  Pallas kernels  54.9 us (97%)
  between operations  1.28 us (2%)
    pallas_call x1, Pallas kernels, forecast(): pl.pallas_call(functools.partial(forecast_kernel, nz, 128 * n_gx * n_gy),...  49.2 us
    pallas_call x1, Pallas kernels, transform(): pl.pallas_call(functools.partial(transform_kernel, piece_rows - 1), out_s...  5.68 us

profile of v4, /device:TPU:1, one launch (start us, length us, event | category | flops | bytes accessed | tf_op | source)
XLA Modules:
  0.0 56.2 jit_solution(13873030167859691918)
XLA Ops:
  1.3 49.2 %shard_map.77 = (f32[8,17,128]{2,1,0:T(8,128)S(1)}, bf16[4096,256]{1,0:T(8,128)(2,1)S(1)}, f32[64,64]{1,0:T(8,128)S(1)}) custom-call(bf16[4096,128]{1,0:T(8,128)(2,1)} %bitcast.5, f32[2,64,64]{2,1,0:T(8,128)} %courant_hbm.1, s32[1,128]{1,0:T(1,128)} %bitcast.6, s32[1,1]{1,0:T(1,128)S(6)} %copy.8.count_ref, f32[1,128]{1,0:T(1,128)} %bitcast.7, f32[1,128]{1,0:T(1,128)} %bitcast.8), custom_call_target="tpu_custom_call" | custom-call | tf_op jit(solution)/shard_map/pallas_call | solution.py:504
  50.5 5.7 %shard_map.78 = (f32[64,64]{1,0:T(8,128)}, bf16[4096,128]{1,0:T(8,128)(2,1)}) custom-call(f32[8,17,128]{2,1,0:T(8,128)S(1)} %get-tuple-element.7.gram_ref, bf16[4096,256]{1,0:T(8,128)(2,1)S(1)} %get-tuple-element.8.anom_hbm, f32[64,64]{1,0:T(8,128)S(1)} %get-tuple-element.9.mean_ref), custom_call_target="tpu_custom_call" | custom-call | tf_op jit(solution)/shard_map/pallas_call | solution.py:135

commit v5 on v4

--- a/solution.py
+++ b/solution.py
@@ -293,11 +293,16 @@
             def _():
                 halo_copy(step, side).start()
 
-    def finish_halo(step):
+    def await_halo(step, sides):
+        for side in sides:
+            @pl.when(there[side])
+            def _():
+                halo_copy(step, side ^ 1).wait_recv()
+
+    def await_sent(step):
         for side in range(4):
             @pl.when(there[side])
             def _():
-                halo_copy(step, side ^ 1).wait_recv()
                 halo_copy(step, side).wait_send()
 
     start_halo(0, (0, 1))
@@ -350,7 +355,9 @@
         states[step][column(SIDE), :] = column_in[step, 1]
 
     def advance_ends(step):
+        await_halo(step, (2, 3))
         place_columns(step)
+        await_halo(step, (0, 1))
         advance_row(step, 0)
         advance_row(step, SIDE - 1)
 
@@ -361,7 +368,6 @@
         lax.fori_loop(1, SIDE - 1, body, 0, unroll=2)
 
     for step in range(STEPS - 1):
-        finish_halo(step)
         advance_ends(step)
         start_halo(step + 1, (0, 1))
         column_out[step + 1, 0] = advance_column(step, 0)
@@ -379,7 +385,6 @@
 
     final = STEPS - 1
     interior(final)
-    finish_halo(final)
     advance_ends(final)
     for cell in (0, SIDE - 1):
         states[STEPS][column(cell), :] = advance_column(final, cell) * last_scale
@@ -486,6 +491,8 @@
     back_end()
     gram_out[...] = whole[...]
     store.wait()
+    for step in range(STEPS):
+        await_sent(step)
 
 
 def keep(array):

time: 56.4 us -> 56.2 us (level)
  no operation moved by 1% of the time
where the time goes in v5:
time: 56.2 us; the launch traced here: 56 us
  Pallas kernels  54.7 us (97%)
  between operations  1.28 us (2%)
    pallas_call x1, Pallas kernels, forecast(): pl.pallas_call(functools.partial(forecast_kernel, nz, 128 * n_gx * n_gy),...  49 us
    pallas_call x1, Pallas kernels, transform(): pl.pallas_call(functools.partial(transform_kernel, piece_rows - 1), out_s...  5.69 us

profile of v5, /device:TPU:1, one launch (start us, length us, event | category | flops | bytes accessed | tf_op | source)
XLA Modules:
  0.0 56.0 jit_solution(14034694010902273932)
XLA Ops:
  1.3 49.0 %shard_map.77 = (f32[8,17,128]{2,1,0:T(8,128)S(1)}, bf16[4096,256]{1,0:T(8,128)(2,1)S(1)}, f32[64,64]{1,0:T(8,128)S(1)}) custom-call(bf16[4096,128]{1,0:T(8,128)(2,1)} %bitcast.5, f32[2,64,64]{2,1,0:T(8,128)} %courant_hbm.1, s32[1,128]{1,0:T(1,128)} %bitcast.6, s32[1,1]{1,0:T(1,128)S(6)} %copy.8.count_ref, f32[1,128]{1,0:T(1,128)} %bitcast.7, f32[1,128]{1,0:T(1,128)} %bitcast.8), custom_call_target="tpu_custom_call" | custom-call | tf_op jit(solution)/shard_map/pallas_call | solution.py:511
  50.3 5.7 %shard_map.78 = (f32[64,64]{1,0:T(8,128)}, bf16[4096,128]{1,0:T(8,128)(2,1)}) custom-call(f32[8,17,128]{2,1,0:T(8,128)S(1)} %get-tuple-element.7.gram_ref, bf16[4096,256]{1,0:T(8,128)(2,1)S(1)} %get-tuple-element.8.anom_hbm, f32[64,64]{1,0:T(8,128)S(1)} %get-tuple-element.9.mean_ref), custom_call_target="tpu_custom_call" | custom-call | tf_op jit(solution)/shard_map/pallas_call | solution.py:135
